TPU v7x, 512 devices: a whole 4x8x8 slice. The times are simulated.
512 devices in a mesh: gx: 8 (over z), gy: 8 (over y), gz: 8 (over x, core).
Axes of the slice: x: 4, y: 8, z: 8, core: 2. Of those that a mesh axis runs over, the one named last changes fastest.
Arguments:
- levels: int32 [64, 64, 1024], P('gx', 'gy', 'gz'), may hold values from 1 to 255
- residual: float32 [3, 64, 64, 1024], P(None, 'gx', 'gy', 'gz'), may hold values from -4 to 4
Outputs:
- correction: float32 [3, 64, 64, 1024], P(None, 'gx', 'gy', 'gz')
- coarse: float32 [3, 32, 32, 512], P(None, 'gx', 'gy', 'gz')
All inputs are finite; a program needn't handle non-finite values.
Results may differ from a plain program's by a relative error of at most 0.00002.
Values sent between devices are 32-bit elements; how exact they have to be, the bound alone decides.
No kernel may reach another device: no remote copies, remote signals or barrier semaphores. Data moves between devices by JAX's collectives and lax.ppermute only.
A program may use at most 128 MiB of HBM per device.

v0:
```python
import functools

import jax
import jax.numpy as jnp
from jax import lax
from jax.experimental import pallas as pl
from jax.experimental.pallas import tpu as pltpu
from jax.sharding import PartitionSpec as P

SWEEPS = 4
THETA = 1.15
DELTA = 0.85

FACE, SIDE, EDGE, FLAT, TURN, TWIST = 9.6, 6.0, 2.7, 1.8, 0.9, 0.4
UNIT = 120.0
WHOLE = 1.92
HALO = 16


def sweep_scales():
    sigma = THETA / DELTA
    rho = 1.0 / sigma
    scales = []
    for _ in range(SWEEPS - 1):
        rho_next = 1.0 / (2.0 * sigma - rho)
        scales.append((rho_next * rho, 2.0 * rho_next / DELTA))
        rho = rho_next
    return scales


def lane_index():
    return lax.broadcasted_iota(jnp.int32, (8, 128), 1)


def join_lanes(centre, above, below):
    up = [pltpu.roll(a, 127, 1) for a in above]
    down = [pltpu.roll(b, 1, 1) for b in below]
    if len(centre) == 2:
        lane = lane_index()
        last, first = lane == 127, lane == 0
        up = [jnp.where(last, up[1], up[0]), jnp.where(last, up[0], up[1])]
        down = [jnp.where(first, down[1], down[0]), jnp.where(first, down[0], down[1])]
    return [c + (u + d) for c, u, d in zip(centre, up, down)]


def stencil(field, plane, row, tiles):
    centre, above, below = [[], [], []], [[], [], []], [[], [], []]
    for tile in range(tiles):
        flat, even, odd = [None] * 3, [None] * 3, [None] * 3
        turn = [None] * 2
        sums = []
        for c in range(3):
            def at(dx, dy):
                return field[c, plane + dx, tile, pl.ds(row + dy, 8), :]

            u = at(0, 0)
            xp, xm, yp, ym = at(1, 0), at(-1, 0), at(0, 1), at(0, -1)
            pp, pm, mp, mm = at(1, 1), at(1, -1), at(-1, 1), at(-1, -1)
            sx, sy = xp + xm, yp + ym
            a, b = pp + mm, pm + mp
            sxy = a + b
            if c < 2:
                dxy = a - b
                turn[c] = dxy
            e, f = pp - mm, pm - mp
            if c != 1:
                dx_sy = e + f
                dx = xp - xm
            if c != 0:
                dy_sx = e - f
                dy = yp - ym
            if c == 0:
                even[0] = SIDE * u + EDGE * sx + FLAT * sy + sxy
                flat[0] = FACE * sx + SIDE * sy + EDGE * sxy
                sums.append((dx, dx_sy))
            elif c == 1:
                even[1] = SIDE * u + EDGE * sy + FLAT * sx + sxy
                flat[1] = FACE * sy + SIDE * sx + EDGE * sxy
                sums.append((dy, dy_sx))
            else:
                both = sx + sy
                even[2] = FACE * u + EDGE * both + sxy
                flat[2] = SIDE * both + FLAT * sxy
                odd[0] = TURN * dx + TWIST * dx_sy
                odd[1] = TURN * dy + TWIST * dy_sx
        odd[2] = TURN * (sums[0][0] + sums[1][0]) + TWIST * (sums[0][1] + sums[1][1])
        even[0] = even[0] + TWIST * turn[1]
        flat[0] = flat[0] + TURN * turn[1]
        even[1] = even[1] + TWIST * turn[0]
        flat[1] = flat[1] + TURN * turn[0]
        for c in range(3):
            centre[c].append(flat[c])
            above[c].append(even[c] + odd[c])
            below[c].append(even[c] - odd[c])
    return [join_lanes(centre[c], above[c], below[c]) for c in range(3)]


def coupling(field, scaled, modulus, plane, row, tiles):
    plain = stencil(field, plane, row, tiles)
    heavy = stencil(scaled, plane, row, tiles)
    return [[modulus[t] * plain[c][t] + heavy[c][t] for t in range(tiles)] for c in range(3)]


def diagonal(modulus, plane, row, tiles):
    centre, even = [], []
    mids = []
    for tile in range(tiles):
        def at(dx, dy):
            return modulus[plane + dx, tile, pl.ds(row + dy, 8), :]

        u = at(0, 0)
        cross = (at(1, 0) + at(-1, 0)) + (at(0, 1) + at(0, -1))
        corner = (at(1, 1) + at(-1, -1)) + (at(1, -1) + at(-1, 1))
        even.append(0.16 * u + 0.06 * cross + 0.03 * corner)
        centre.append(WHOLE * u + 0.16 * cross + 0.06 * corner)
        mids.append(u)
    total = join_lanes(centre, even, even)
    out = []
    for tile in range(tiles):
        diag = (1.05 * 0.5 * UNIT) * total[tile]
        inside = mids[tile] > 0.0
        inverse = jnp.where(inside, 1.0 / jnp.where(inside, diag, 1.0), 0.0)
        out.append((mids[tile], diag, inverse))
    return out


def pair_matrix(shape, fine_axis):
    fine = lax.broadcasted_iota(jnp.int32, shape, fine_axis)
    coarse = lax.broadcasted_iota(jnp.int32, shape, 1 - fine_axis)
    return (lax.shift_right_logical(fine, 1) == coarse).astype(jnp.float32)


def prepare(levels, residual, main, first, last):
    lane = lane_index()
    for c in range(4):
        head = jnp.zeros((8, 128), jnp.float32)
        tail = jnp.zeros((8, 128), jnp.float32)
        for p in range(8):
            if c < 3:
                value = residual[c, p]
            else:
                ratio = levels[p].astype(jnp.float32) / 255.0
                value = (0.05 + 0.95 * ratio * ratio * ratio) / UNIT
            main[c, p] = value
            mine = (lane >= HALO * p) & (lane < HALO * (p + 1))
            head = jnp.where(mine, pltpu.roll(value, HALO * p, 1) if p else value, head)
            tail = jnp.where(mine, pltpu.roll(value, (HALO * p + HALO) % 128, 1) if p < 7 else value, tail)
        first[c, 0] = head
        last[c, 0] = tail


def smooth_kernel(down, own, up, smooth, message, state, u, v, rest, modulus, diag, inverse, pairs):
    lane = lane_index()
    low, high = lane < HALO, lane >= 128 - HALO

    for t, block in enumerate((down, own, up)):
        def place(b, carry, t=t, block=block):
            for c in range(4):
                left, right = block[b, c, 8], block[b, c, 9]
                for p in range(8):
                    side_r = pltpu.roll(right, 128 - HALO * p, 1) if p else right
                    side_l = pltpu.roll(left, 112 - HALO * p, 1) if p < 7 else left
                    side = jnp.where(low, side_r, jnp.where(high, side_l, 0.0))
                    if c < 3:
                        rest[c, 8 * b + p, 0, pl.ds(8 * t, 8), :] = block[b, c, p]
                        rest[c, 8 * b + p, 1, pl.ds(8 * t, 8), :] = side
                    else:
                        modulus[8 * b + p, 0, pl.ds(8 + 8 * t, 8), :] = block[b, c, p]
                        modulus[8 * b + p, 1, pl.ds(8 + 8 * t, 8), :] = side
            return carry

        lax.fori_loop(0, 3, place, 0)

    def begin(plane, carry):
        for t in range(3):
            parts = diagonal(modulus, plane, 8 + 8 * t, 2)
            for tile, (mid, d, inv) in enumerate(parts):
                diag[plane, tile, pl.ds(8 * t, 8), :] = d
                inverse[plane, tile, pl.ds(8 * t, 8), :] = inv
                for c in range(3):
                    step = rest[c, plane, tile, pl.ds(8 * t, 8), :] * (inv * (1.0 / THETA))
                    u[0, c, plane, tile, pl.ds(8 + 8 * t, 8), :] = step
                    v[0, c, plane, tile, pl.ds(8 + 8 * t, 8), :] = mid * step
        return carry

    lax.fori_loop(1, 23, begin, 0)

    def gather(slot, start):
        def body(p, carry):
            for c in range(3):
                step = u[slot, c, 8 + p, 0, pl.ds(16, 8), :]
                smooth[c, p] = step if start else smooth[c, p] + step
            return carry

        lax.fori_loop(0, 8, body, 0)

    gather(0, True)
    scales = sweep_scales()
    for k in range(1, SWEEPS + 1):
        now, later = (k - 1) % 2, k % 2
        rows = (0, 8, 16) if k < 3 else (4, 12)

        def sweep(plane, carry, k=k, now=now, later=later, rows=rows):
            for row in rows:
                mod = [modulus[plane, tile, pl.ds(8 + row, 8), :] for tile in range(2)]
                out = coupling(u.at[now], v.at[now], mod, plane, 8 + row, 2)
                for tile in range(2):
                    d = diag[plane, tile, pl.ds(row, 8), :]
                    if k < SWEEPS:
                        keep, push = scales[k - 1]
                        inv = inverse[plane, tile, pl.ds(row, 8), :] * push
                    for c in range(3):
                        old = u[now, c, plane, tile, pl.ds(8 + row, 8), :]
                        r = rest[c, plane, tile, pl.ds(row, 8), :] - d * old + out[c][tile]
                        rest[c, plane, tile, pl.ds(row, 8), :] = r
                        if k < SWEEPS:
                            step = keep * old + inv * r
                            u[later, c, plane, tile, pl.ds(8 + row, 8), :] = step
                            v[later, c, plane, tile, pl.ds(8 + row, 8), :] = mod[tile] * step
            return carry

        lax.fori_loop(1 + k if k < SWEEPS else 5, 23 - k if k < SWEEPS else 19, sweep, 0)
        if k < SWEEPS:
            gather(later, False)

    def restrict(p, carry):
        for tile in range(2):
            for c in range(4):
                total = None
                for dx in range(2):
                    for dy in range(2):
                        if c < 3:
                            part = rest[c, 4 + 2 * p + dx, tile, pl.ds(4 + dy, 8, stride=2), :]
                        else:
                            part = 0.25 * modulus[4 + 2 * p + dx, tile, pl.ds(12 + dy, 8, stride=2), :]
                        total = part if total is None else total + part
                pairs[tile, c, p] = total
        return carry

    lax.fori_loop(0, 8, restrict, 0)
    matrix = pair_matrix((256, 128), 0)
    coarse = jnp.dot(
        pairs[0].reshape(256, 128),
        matrix[:128],
        precision=lax.Precision.HIGHEST,
        preferred_element_type=jnp.float32,
    ) + jnp.dot(
        pairs[1].reshape(256, 128),
        matrix[128:],
        precision=lax.Precision.HIGHEST,
        preferred_element_type=jnp.float32,
    )
    message[...] = coarse.reshape(4, 8, 8, 128)

    def keep_state(p, carry):
        for tile in range(2):
            for c in range(3):
                state[c, p, tile] = rest[c, 4 + p, tile, pl.ds(4, 16), :]
            state[3, p, tile] = modulus[4 + p, tile, pl.ds(12, 16), :]
            state[4, p, tile] = diag[4 + p, tile, pl.ds(4, 16), :]
            state[5, p, tile] = inverse[4 + p, tile, pl.ds(4, 16), :]
        return carry

    lax.fori_loop(0, 16, keep_state, 0)


def post_kernel(down, own, up, state, smooth, correction, coarse, cu, cv, crest, cmod, cinv, cdiag, total, u, v, wide):
    scales = sweep_scales()

    def place(p, carry):
        for c in range(4):
            below, mid, above = down[c, p], own[c, p, pl.ds(2, 4), :], up[c, p]
            if c < 3:
                crest[c, p, 0, pl.ds(0, 8), :] = below
                crest[c, p, 0, pl.ds(8, 8), :] = above
                crest[c, p, 0, pl.ds(6, 4), :] = mid
            else:
                cmod[p, 0, pl.ds(8, 8), :] = below
                cmod[p, 0, pl.ds(16, 8), :] = above
                cmod[p, 0, pl.ds(14, 4), :] = mid
        return carry

    lax.fori_loop(0, 16, place, 0)

    def begin(plane, carry):
        for t in range(2):
            mid, d, inv = diagonal(cmod, plane, 8 + 8 * t, 1)[0]
            cdiag[plane, 0, pl.ds(8 * t, 8), :] = d
            cinv[plane, 0, pl.ds(8 * t, 8), :] = inv
            for c in range(3):
                step = crest[c, plane, 0, pl.ds(8 * t, 8), :] * (inv * (1.0 / THETA))
                cu[0, c, plane, 0, pl.ds(8 + 8 * t, 8), :] = step
                cv[0, c, plane, 0, pl.ds(8 + 8 * t, 8), :] = mid * step
        return carry

    lax.fori_loop(1, 15, begin, 0)

    def gather(slot, start):
        def body(p, carry):
            for c in range(3):
                step = cu[slot, c, 4 + p, 0, pl.ds(12, 8), :]
                total[c, p] = step if start else total[c, p] + step
            return carry

        lax.fori_loop(0, 8, body, 0)

    gather(0, True)
    for k in range(1, SWEEPS):
        now, later = (k - 1) % 2, k % 2

        def sweep(plane, carry, k=k, now=now, later=later):
            for row in (0, 8):
                mod = [cmod[plane, 0, pl.ds(8 + row, 8), :]]
                out = coupling(cu.at[now], cv.at[now], mod, plane, 8 + row, 1)
                d = cdiag[plane, 0, pl.ds(row, 8), :]
                keep, push = scales[k - 1]
                inv = cinv[plane, 0, pl.ds(row, 8), :] * push
                for c in range(3):
                    old = cu[now, c, plane, 0, pl.ds(8 + row, 8), :]
                    r = crest[c, plane, 0, pl.ds(row, 8), :] - d * old + out[c][0]
                    crest[c, plane, 0, pl.ds(row, 8), :] = r
                    step = keep * old + inv * r
                    cu[later, c, plane, 0, pl.ds(8 + row, 8), :] = step
                    cv[later, c, plane, 0, pl.ds(8 + row, 8), :] = mod[0] * step
            return carry

        lax.fori_loop(1 + k, 15 - k, sweep, 0)
        gather(later, False)

    for c in range(3):
        for p in range(4):
            coarse[c, p] = total[c, 2 + p, pl.ds(2, 4), pl.ds(0, 64)]

    matrix = pair_matrix((128, 256), 1)
    for tile in range(2):
        spread = jnp.dot(
            total[...].reshape(192, 128),
            matrix[:, 128 * tile : 128 * (tile + 1)],
            precision=lax.Precision.HIGHEST,
            preferred_element_type=jnp.float32,
        )
        wide[tile] = spread.reshape(3, 8, 8, 128)

    def lift(p, carry):
        for tile in range(2):
            for c in range(3):
                value = wide[tile, c, p]
                for dx in range(2):
                    for dy in range(2):
                        u[0, c, 2 * p + dx, tile, pl.ds(8 + dy, 8, stride=2), :] = value
        return carry

    lax.fori_loop(0, 8, lift, 0)

    def weigh(p, carry):
        for tile in range(2):
            mod = state[3, p, tile]
            for c in range(3):
                v[0, c, p, tile, pl.ds(8, 16), :] = mod * u[0, c, p, tile, pl.ds(8, 16), :]
        return carry

    lax.fori_loop(0, 16, weigh, 0)

    def add_own(slot, start):
        def body(p, carry):
            for c in range(3):
                step = u[slot, c, 4 + p, 0, pl.ds(12, 8), :]
                correction[c, p] = (smooth[c, p] if start else correction[c, p]) + step
            return carry

        lax.fori_loop(0, 8, body, 0)

    add_own(0, True)
    for k in range(SWEEPS):
        now, later = k % 2, (k + 1) % 2
        rows = (0, 8) if k < SWEEPS - 1 else (4,)

        def sweep(plane, carry, k=k, now=now, later=later, rows=rows):
            for row in rows:
                mod = [state[3, plane, tile, pl.ds(row, 8), :] for tile in range(2)]
                out = coupling(u.at[now], v.at[now], mod, plane, 8 + row, 2)
                for tile in range(2 if k < SWEEPS - 1 else 1):
                    d = state[4, plane, tile, pl.ds(row, 8), :]
                    keep, push = scales[k - 1] if k else (None, 1.0 / THETA)
                    inv = state[5, plane, tile, pl.ds(row, 8), :] * push
                    for c in range(3):
                        old = u[now, c, plane, tile, pl.ds(8 + row, 8), :]
                        r = state[c, plane, tile, pl.ds(row, 8), :] - d * old + out[c][tile]
                        step = inv * r
                        if k:
                            step = keep * old + step
                        if k < SWEEPS - 1:
                            state[c, plane, tile, pl.ds(row, 8), :] = r
                            u[later, c, plane, tile, pl.ds(8 + row, 8), :] = step
                            v[later, c, plane, tile, pl.ds(8 + row, 8), :] = mod[tile] * step
                        else:
                            correction[c, plane - 4] = correction[c, plane - 4] + step
            return carry

        lax.fori_loop(1 + k, 15 - k, sweep, 0)
        if k < SWEEPS - 1:
            add_own(later, False)


def call(kernel, outs, scratch=(), aliases=None):
    return pl.pallas_call(
        kernel,
        out_shape=[jax.ShapeDtypeStruct(s, jnp.float32) for s in outs],
        scratch_shapes=[pltpu.VMEM(s, jnp.float32) for s in scratch],
        input_output_aliases=aliases or {},
        compiler_params=pltpu.CompilerParams(vmem_limit_bytes=48 * 1024 * 1024),
    )


def neighbours(to_next, to_previous, axis):
    count = lax.axis_size(axis)
    before = lax.ppermute(to_next, axis, [(i, i + 1) for i in range(count - 1)])
    after = lax.ppermute(to_previous, axis, [(i + 1, i) for i in range(count - 1)])
    return before, after


def on_device(levels, residual):
    main, first, last = call(prepare, [(4, 8, 8, 128), (4, 1, 8, 128), (4, 1, 8, 128)])(levels, residual)
    left, right = neighbours(last, first, "gz")
    block = jnp.concatenate([main, left, right], axis=1)
    before, after = neighbours(block, block, "gx")
    slab = jnp.stack([before, block, after])
    down, up = neighbours(slab, slab, "gy")
    planes, rows = 24, 24
    smooth, message, state = call(
        smooth_kernel,
        [(3, 8, 8, 128), (4, 8, 8, 128), (6, 16, 2, 16, 128)],
        [
            (2, 3, planes, 2, rows + 16, 128),
            (2, 3, planes, 2, rows + 16, 128),
            (3, planes, 2, rows, 128),
            (planes, 2, rows + 16, 128),
            (planes, 2, rows, 128),
            (planes, 2, rows, 128),
            (2, 4, 8, 8, 128),
        ],
    )(down, slab, up)
    before, after = neighbours(message, message, "gx")
    slab = jnp.concatenate([before[:, :6], message[:, 2:6], after[:, 2:]], axis=1)
    down, up = neighbours(slab, slab, "gy")
    correction, coarse = call(
        functools.partial(post_outer),
        [(3, 8, 8, 128), (3, 4, 4, 64)],
        [
            (2, 3, 16, 1, 32, 128),
            (2, 3, 16, 1, 32, 128),
            (3, 16, 1, 16, 128),
            (16, 1, 32, 128),
            (16, 1, 16, 128),
            (16, 1, 16, 128),
            (3, 8, 8, 128),
            (2, 3, 16, 2, 32, 128),
            (2, 3, 16, 2, 32, 128),
            (2, 3, 8, 8, 128),
            (6, 16, 2, 16, 128),
        ],
    )(down, slab, up, state, smooth)
    return correction, coarse


def post_outer(down, own, up, state_in, smooth, correction, coarse, *scratch):
    state = scratch[-1]

    def copy(p, carry):
        for f in range(6):
            state[f, p] = state_in[f, p]
        return carry

    lax.fori_loop(0, 16, copy, 0)
    post_kernel(down, own, up, state, smooth, correction, coarse, *scratch[:-1])


def solution(mesh):
    return jax.shard_map(
        on_device,
        mesh=mesh,
        in_specs=(P("gx", "gy", "gz"), P(None, "gx", "gy", "gz")),
        out_specs=(P(None, "gx", "gy", "gz"), P(None, "gx", "gy", "gz")),
        check_vma=False,
    )
```

profile of v0, /device:TPU:288, one launch (start us, length us, event | category | flops | bytes accessed | tf_op | source)
XLA Modules:
  0.0 96.1 jit_solution(14378639145234811525)
XLA Ops:
  0.6 0.9 copy-done
  1.5 0.8 copy-done.1
  2.3 0.1 shard_map.41
  2.4 1.7 %collective-permute-start = (f32[4,1,8,128]{3,2,1,0:T(8,128)S(1)}, f32[4,1,8,128]{3,2,1,0:T(8,128)S(1)}, u32[]{:S(2)}, u32[]{:S(2)}) collective-permute-start(f32[4,1,8,128]{3,2,1,0:T(8,128)S(1)} %get-tuple-element.9), channel_id=1, source_target_pairs={{0,1},{1,2},{2,3},{3,4},{4,5},{5,6},{6,7},{8,9},{9,10},{10,11},{11... | collective-permute-start | bytes 49160 | tf_op jit(solution)/shard_map/ppermute | solution.py:417
  4.2 1.3 %collective-permute-start.1 = (f32[4,1,8,128]{3,2,1,0:T(8,128)S(1)}, f32[4,1,8,128]{3,2,1,0:T(8,128)S(1)}, u32[]{:S(2)}, u32[]{:S(2)}) collective-permute-start(f32[4,1,8,128]{3,2,1,0:T(8,128)S(1)} %get-tuple-element.10), channel_id=1, source_target_pairs={{1,0},{2,1},{3,2},{4,3},{5,4},{6,5},{7,6},{9,8},{10,9},{11,10},{12... | collective-permute-start | bytes 49160 | tf_op jit(solution)/shard_map/ppermute | solution.py:418
  5.5 3.0 %collective-permute-done.1 = f32[4,1,8,128]{3,2,1,0:T(8,128)S(1)} collective-permute-done((f32[4,1,8,128]{3,2,1,0:T(8,128)S(1)}, f32[4,1,8,128]{3,2,1,0:T(8,128)S(1)}, u32[]{:S(2)}, u32[]{:S(2)}) %collective-permute-start.1) | collective-permute-done | bytes 16416 | tf_op jit(solution)/shard_map/ppermute | solution.py:418
  8.5 1.9 %collective-permute-start.3 = (f32[4,10,8,128]{3,2,1,0:T(8,128)S(1)}, f32[4,10,8,128]{3,2,1,0:T(8,128)S(1)}, u32[]{:S(2)}, u32[]{:S(2)}) collective-permute-start(f32[4,10,8,128]{3,2,1,0:T(8,128)S(1)} %constant_dynamic-update-slice_fusion), channel_id=1, source_target_pairs={{64,0},{128,64},{192,128},{256,192},{320,256},{384,320},{448,384},... | collective-permute-start | bytes 491528 | tf_op jit(solution)/shard_map/ppermute | solution.py:418
  10.4 3.9 %collective-permute-start.2 = (f32[4,10,8,128]{3,2,1,0:T(8,128)S(1)}, f32[4,10,8,128]{3,2,1,0:T(8,128)S(1)}, u32[]{:S(2)}, u32[]{:S(2)}) collective-permute-start(f32[4,10,8,128]{3,2,1,0:T(8,128)S(1)} %constant_dynamic-update-slice_fusion), channel_id=1, source_target_pairs={{0,64},{64,128},{128,192},{192,256},{256,320},{320,384},{384,448},... | collective-permute-start | bytes 491528 | tf_op jit(solution)/shard_map/ppermute | solution.py:417
  14.4 1.5 %collective-permute-done.3 = f32[4,10,8,128]{3,2,1,0:T(8,128)S(1)} collective-permute-done((f32[4,10,8,128]{3,2,1,0:T(8,128)S(1)}, f32[4,10,8,128]{3,2,1,0:T(8,128)S(1)}, u32[]{:S(2)}, u32[]{:S(2)}) %collective-permute-start.3) | collective-permute-done | bytes 163872 | tf_op jit(solution)/shard_map/ppermute | solution.py:418
  15.9 3.1 %collective-permute-done.2 = f32[4,10,8,128]{3,2,1,0:T(8,128)S(1)} collective-permute-done((f32[4,10,8,128]{3,2,1,0:T(8,128)S(1)}, f32[4,10,8,128]{3,2,1,0:T(8,128)S(1)}, u32[]{:S(2)}, u32[]{:S(2)}) %collective-permute-start.2) | collective-permute-done | bytes 163872 | tf_op jit(solution)/shard_map/ppermute | solution.py:417
  19.1 2.4 %collective-permute-start.5 = (f32[3,4,10,8,128]{4,3,2,1,0:T(8,128)S(1)}, f32[3,4,10,8,128]{4,3,2,1,0:T(8,128)S(1)}, u32[]{:S(2)}, u32[]{:S(2)}) collective-permute-start(f32[3,4,10,8,128]{4,3,2,1,0:T(8,128)S(1)} %pad_maximum_fusion.own), channel_id=1, source_target_pairs={{8,0},{16,8},{24,16},{32,24},{40,32},{48,40},{56,48},{9,1},{17,9},... | collective-permute-start | bytes 1474568 | tf_op jit(solution)/shard_map/ppermute | solution.py:418
  21.4 3.5 %collective-permute-start.4 = (f32[3,4,10,8,128]{4,3,2,1,0:T(8,128)S(1)}, f32[3,4,10,8,128]{4,3,2,1,0:T(8,128)S(1)}, u32[]{:S(2)}, u32[]{:S(2)}) collective-permute-start(f32[3,4,10,8,128]{4,3,2,1,0:T(8,128)S(1)} %pad_maximum_fusion.own), channel_id=1, source_target_pairs={{0,8},{8,16},{16,24},{24,32},{32,40},{40,48},{48,56},{1,9},{9,17},... | collective-permute-start | bytes 1474568 | tf_op jit(solution)/shard_map/ppermute | solution.py:417
  24.9 9.8 %collective-permute-done.5.up = f32[3,4,10,8,128]{4,3,2,1,0:T(8,128)S(1)} collective-permute-done((f32[3,4,10,8,128]{4,3,2,1,0:T(8,128)S(1)}, f32[3,4,10,8,128]{4,3,2,1,0:T(8,128)S(1)}, u32[]{:S(2)}, u32[]{:S(2)}) %collective-permute-start.5) | collective-permute-done | bytes 491552 | tf_op jit(solution)/shard_map/ppermute | solution.py:418
  34.7 3.8 %collective-permute-done.4.down = f32[3,4,10,8,128]{4,3,2,1,0:T(8,128)S(1)} collective-permute-done((f32[3,4,10,8,128]{4,3,2,1,0:T(8,128)S(1)}, f32[3,4,10,8,128]{4,3,2,1,0:T(8,128)S(1)}, u32[]{:S(2)}, u32[]{:S(2)}) %collective-permute-start.4) | collective-permute-done | bytes 491552 | tf_op jit(solution)/shard_map/ppermute | solution.py:417
  38.5 18.0 %shard_map.42 = (f32[3,8,8,128]{3,2,1,0:T(8,128)S(1)}, f32[4,8,8,128]{3,2,1,0:T(8,128)S(1)}, f32[6,16,2,16,128]{4,3,2,1,0:T(8,128)S(1)}) custom-call(f32[3,4,10,8,128]{4,3,2,1,0:T(8,128)S(1)} %collective-permute-done.4.down, f32[3,4,10,8,128]{4,3,2,1,0:T(8,128)S(1)} %pad_maximum_fusion.own, f32[3,4,10,8,128]{4,3,2,1,0:T(8,128)S(1)} %collective-permute-done.5.up), custom_call_target="tpu_custom_call" | custom-call | tf_op jit(solution)/shard_map/pallas_call | solution.py:430
  56.5 1.9 %collective-permute-start.7 = (f32[4,8,8,128]{3,2,1,0:T(8,128)S(1)}, f32[4,8,8,128]{3,2,1,0:T(8,128)S(1)}, u32[]{:S(2)}, u32[]{:S(2)}) collective-permute-start(f32[4,8,8,128]{3,2,1,0:T(8,128)S(1)} %get-tuple-element.11), channel_id=1, source_target_pairs={{64,0},{128,64},{192,128},{256,192},{320,256},{384,320},{448,384},... | collective-permute-start | bytes 393224 | tf_op jit(solution)/shard_map/ppermute | solution.py:418
  58.5 3.9 %collective-permute-start.6 = (f32[4,8,8,128]{3,2,1,0:T(8,128)S(1)}, f32[4,8,8,128]{3,2,1,0:T(8,128)S(1)}, u32[]{:S(2)}, u32[]{:S(2)}) collective-permute-start(f32[4,8,8,128]{3,2,1,0:T(8,128)S(1)} %get-tuple-element.11), channel_id=1, source_target_pairs={{0,64},{64,128},{128,192},{192,256},{256,320},{320,384},{384,448},... | collective-permute-start | bytes 393224 | tf_op jit(solution)/shard_map/ppermute | solution.py:417
  62.4 1.5 %collective-permute-done.7 = f32[4,8,8,128]{3,2,1,0:T(8,128)S(1)} collective-permute-done((f32[4,8,8,128]{3,2,1,0:T(8,128)S(1)}, f32[4,8,8,128]{3,2,1,0:T(8,128)S(1)}, u32[]{:S(2)}, u32[]{:S(2)}) %collective-permute-start.7) | collective-permute-done | bytes 131104 | tf_op jit(solution)/shard_map/ppermute | solution.py:418
  64.0 3.1 %collective-permute-done.6 = f32[4,8,8,128]{3,2,1,0:T(8,128)S(1)} collective-permute-done((f32[4,8,8,128]{3,2,1,0:T(8,128)S(1)}, f32[4,8,8,128]{3,2,1,0:T(8,128)S(1)}, u32[]{:S(2)}, u32[]{:S(2)}) %collective-permute-start.6) | collective-permute-done | bytes 131104 | tf_op jit(solution)/shard_map/ppermute | solution.py:417
  67.1 1.9 %collective-permute-start.9 = (f32[4,16,8,128]{3,2,1,0:T(8,128)S(1)}, f32[4,16,8,128]{3,2,1,0:T(8,128)S(1)}, u32[]{:S(2)}, u32[]{:S(2)}) collective-permute-start(f32[4,16,8,128]{3,2,1,0:T(8,128)S(1)} %pad_maximum_fusion.1.own), channel_id=1, source_target_pairs={{8,0},{16,8},{24,16},{32,24},{40,32},{48,40},{56,48},{9,1},{17,9},... | collective-permute-start | bytes 786440 | tf_op jit(solution)/shard_map/ppermute | solution.py:418
  69.1 3.9 %collective-permute-start.8 = (f32[4,16,8,128]{3,2,1,0:T(8,128)S(1)}, f32[4,16,8,128]{3,2,1,0:T(8,128)S(1)}, u32[]{:S(2)}, u32[]{:S(2)}) collective-permute-start(f32[4,16,8,128]{3,2,1,0:T(8,128)S(1)} %pad_maximum_fusion.1.own), channel_id=1, source_target_pairs={{0,8},{8,16},{16,24},{24,32},{32,40},{40,48},{48,56},{1,9},{9,17},... | collective-permute-start | bytes 786440 | tf_op jit(solution)/shard_map/ppermute | solution.py:417
  73.0 3.5 %collective-permute-done.9.up = f32[4,16,8,128]{3,2,1,0:T(8,128)S(1)} collective-permute-done((f32[4,16,8,128]{3,2,1,0:T(8,128)S(1)}, f32[4,16,8,128]{3,2,1,0:T(8,128)S(1)}, u32[]{:S(2)}, u32[]{:S(2)}) %collective-permute-start.9) | collective-permute-done | bytes 262176 | tf_op jit(solution)/shard_map/ppermute | solution.py:418
  76.5 3.1 %collective-permute-done.8.down = f32[4,16,8,128]{3,2,1,0:T(8,128)S(1)} collective-permute-done((f32[4,16,8,128]{3,2,1,0:T(8,128)S(1)}, f32[4,16,8,128]{3,2,1,0:T(8,128)S(1)}, u32[]{:S(2)}, u32[]{:S(2)}) %collective-permute-start.8) | collective-permute-done | bytes 262176 | tf_op jit(solution)/shard_map/ppermute | solution.py:417
  79.7 16.4 %shard_map.43 = (f32[3,8,8,128]{3,2,1,0:T(8,128)}, f32[3,4,4,64]{3,2,1,0:T(4,128)}) custom-call(f32[4,16,8,128]{3,2,1,0:T(8,128)S(1)} %collective-permute-done.8.down, f32[4,16,8,128]{3,2,1,0:T(8,128)S(1)} %pad_maximum_fusion.1.own, f32[4,16,8,128]{3,2,1,0:T(8,128)S(1)} %collective-permute-done.9.up, f32[6,16,2,16,128]{4,3,2,1,0:T(8,128)S(1)} %get-tuple-element.12.state_in, ...), custom_call_target="tpu_custom_call" | custom-call | tf_op jit(solution)/shard_map/pallas_call | solution.py:446
  (11 shorter events, 0.1 us)
Async XLA Ops:
  0.6 0.9 copy-start
  1.5 0.8 copy-start.1
  2.4 3.1 %collective-permute-start = (f32[4,1,8,128]{3,2,1,0:T(8,128)S(1)}, f32[4,1,8,128]{3,2,1,0:T(8,128)S(1)}, u32[]{:S(2)}, u32[]{:S(2)}) collective-permute-start(f32[4,1,8,128]{3,2,1,0:T(8,128)S(1)} %get-tuple-element.9), channel_id=1, source_target_pairs={{0,1},{1,2},{2,3},{3,4},{4,5},{5,6},{6,7},{8,9},{9,10},{10,11},{11... | collective-permute-start | bytes 49160 | tf_op jit(solution)/shard_map/ppermute | solution.py:417
  4.2 4.4 %collective-permute-start.1 = (f32[4,1,8,128]{3,2,1,0:T(8,128)S(1)}, f32[4,1,8,128]{3,2,1,0:T(8,128)S(1)}, u32[]{:S(2)}, u32[]{:S(2)}) collective-permute-start(f32[4,1,8,128]{3,2,1,0:T(8,128)S(1)} %get-tuple-element.10), channel_id=1, source_target_pairs={{1,0},{2,1},{3,2},{4,3},{5,4},{6,5},{7,6},{9,8},{10,9},{11,10},{12... | collective-permute-start | bytes 49160 | tf_op jit(solution)/shard_map/ppermute | solution.py:418
  8.5 7.4 %collective-permute-start.3 = (f32[4,10,8,128]{3,2,1,0:T(8,128)S(1)}, f32[4,10,8,128]{3,2,1,0:T(8,128)S(1)}, u32[]{:S(2)}, u32[]{:S(2)}) collective-permute-start(f32[4,10,8,128]{3,2,1,0:T(8,128)S(1)} %constant_dynamic-update-slice_fusion), channel_id=1, source_target_pairs={{64,0},{128,64},{192,128},{256,192},{320,256},{384,320},{448,384},... | collective-permute-start | bytes 491528 | tf_op jit(solution)/shard_map/ppermute | solution.py:418
  10.4 8.6 %collective-permute-start.2 = (f32[4,10,8,128]{3,2,1,0:T(8,128)S(1)}, f32[4,10,8,128]{3,2,1,0:T(8,128)S(1)}, u32[]{:S(2)}, u32[]{:S(2)}) collective-permute-start(f32[4,10,8,128]{3,2,1,0:T(8,128)S(1)} %constant_dynamic-update-slice_fusion), channel_id=1, source_target_pairs={{0,64},{64,128},{128,192},{192,256},{256,320},{320,384},{384,448},... | collective-permute-start | bytes 491528 | tf_op jit(solution)/shard_map/ppermute | solution.py:417
  19.1 15.6 %collective-permute-start.5 = (f32[3,4,10,8,128]{4,3,2,1,0:T(8,128)S(1)}, f32[3,4,10,8,128]{4,3,2,1,0:T(8,128)S(1)}, u32[]{:S(2)}, u32[]{:S(2)}) collective-permute-start(f32[3,4,10,8,128]{4,3,2,1,0:T(8,128)S(1)} %pad_maximum_fusion.own), channel_id=1, source_target_pairs={{8,0},{16,8},{24,16},{32,24},{40,32},{48,40},{56,48},{9,1},{17,9},... | collective-permute-start | bytes 1474568 | tf_op jit(solution)/shard_map/ppermute | solution.py:418
  21.4 17.1 %collective-permute-start.4 = (f32[3,4,10,8,128]{4,3,2,1,0:T(8,128)S(1)}, f32[3,4,10,8,128]{4,3,2,1,0:T(8,128)S(1)}, u32[]{:S(2)}, u32[]{:S(2)}) collective-permute-start(f32[3,4,10,8,128]{4,3,2,1,0:T(8,128)S(1)} %pad_maximum_fusion.own), channel_id=1, source_target_pairs={{0,8},{8,16},{16,24},{24,32},{32,40},{40,48},{48,56},{1,9},{9,17},... | collective-permute-start | bytes 1474568 | tf_op jit(solution)/shard_map/ppermute | solution.py:417
  56.5 7.4 %collective-permute-start.7 = (f32[4,8,8,128]{3,2,1,0:T(8,128)S(1)}, f32[4,8,8,128]{3,2,1,0:T(8,128)S(1)}, u32[]{:S(2)}, u32[]{:S(2)}) collective-permute-start(f32[4,8,8,128]{3,2,1,0:T(8,128)S(1)} %get-tuple-element.11), channel_id=1, source_target_pairs={{64,0},{128,64},{192,128},{256,192},{320,256},{384,320},{448,384},... | collective-permute-start | bytes 393224 | tf_op jit(solution)/shard_map/ppermute | solution.py:418
  58.5 8.6 %collective-permute-start.6 = (f32[4,8,8,128]{3,2,1,0:T(8,128)S(1)}, f32[4,8,8,128]{3,2,1,0:T(8,128)S(1)}, u32[]{:S(2)}, u32[]{:S(2)}) collective-permute-start(f32[4,8,8,128]{3,2,1,0:T(8,128)S(1)} %get-tuple-element.11), channel_id=1, source_target_pairs={{0,64},{64,128},{128,192},{192,256},{256,320},{320,384},{384,448},... | collective-permute-start | bytes 393224 | tf_op jit(solution)/shard_map/ppermute | solution.py:417
  67.1 9.4 %collective-permute-start.9 = (f32[4,16,8,128]{3,2,1,0:T(8,128)S(1)}, f32[4,16,8,128]{3,2,1,0:T(8,128)S(1)}, u32[]{:S(2)}, u32[]{:S(2)}) collective-permute-start(f32[4,16,8,128]{3,2,1,0:T(8,128)S(1)} %pad_maximum_fusion.1.own), channel_id=1, source_target_pairs={{8,0},{16,8},{24,16},{32,24},{40,32},{48,40},{56,48},{9,1},{17,9},... | collective-permute-start | bytes 786440 | tf_op jit(solution)/shard_map/ppermute | solution.py:418
  69.1 10.6 %collective-permute-start.8 = (f32[4,16,8,128]{3,2,1,0:T(8,128)S(1)}, f32[4,16,8,128]{3,2,1,0:T(8,128)S(1)}, u32[]{:S(2)}, u32[]{:S(2)}) collective-permute-start(f32[4,16,8,128]{3,2,1,0:T(8,128)S(1)} %pad_maximum_fusion.1.own), channel_id=1, source_target_pairs={{0,8},{8,16},{16,24},{24,32},{32,40},{40,48},{48,56},{1,9},{9,17},... | collective-permute-start | bytes 786440 | tf_op jit(solution)/shard_map/ppermute | solution.py:417
where the time goes:
time: 96.5 us; the launch traced here: 96.1 us
  Pallas kernels  34.6 us (36%)
  waiting for transfers between devices  32.6 us (34%)
  starting transfers between devices  26.4 us (27%)
  local copies, waits for them, and re-layouts  1.68 us (2%)
    ppermute x5, waiting for transfers between devices, neighbours(): lax.ppermute(to_previous, axis, [(i + 1, i) for i in range(count - 1)])  19.4 us
    pallas_call x1, Pallas kernels, on_device(): call(smooth_kernel, [(3, 8, 8, 128), (4, 8, 8, 128), (6, 16, 2, 16, 128)]...  18 us
    ppermute x5, starting transfers between devices, neighbours(): before = lax.ppermute(to_next, axis, [(i, i + 1) for i in range(count - 1)])  17 us
    pallas_call x1, Pallas kernels, on_device(): call(functools.partial(post_outer), [(3, 8, 8, 128), (3, 4, 4, 64)], [(2,...  16.4 us
    ppermute x5, waiting for transfers between devices, neighbours(): before = lax.ppermute(to_next, axis, [(i, i + 1) for i in range(count - 1)])  13.2 us
    ppermute x5, starting transfers between devices, neighbours(): lax.ppermute(to_previous, axis, [(i + 1, i) for i in range(count - 1)])  9.4 us
  transfers between devices with their start and end apart: 10, of which 9 were waited for; matrix products, arithmetic and copies ran while one was open for 0% of the time, Pallas kernels for 0%

commit v1 on v0

--- a/solution.py
+++ b/solution.py
@@ -43,62 +43,96 @@
     return [c + (u + d) for c, u, d in zip(centre, up, down)]
 
 
-def stencil(field, plane, row, tiles):
-    centre, above, below = [[], [], []], [[], [], []], [[], [], []]
+def stencil(field, plane, count, row, tiles):
+    centre = [[[] for _ in range(3)] for _ in range(count)]
+    above = [[[] for _ in range(3)] for _ in range(count)]
+    below = [[[] for _ in range(3)] for _ in range(count)]
     for tile in range(tiles):
-        flat, even, odd = [None] * 3, [None] * 3, [None] * 3
-        turn = [None] * 2
-        sums = []
+        mid, summed, spread = [], [], []
         for c in range(3):
-            def at(dx, dy):
-                return field[c, plane + dx, tile, pl.ds(row + dy, 8), :]
-
-            u = at(0, 0)
-            xp, xm, yp, ym = at(1, 0), at(-1, 0), at(0, 1), at(0, -1)
-            pp, pm, mp, mm = at(1, 1), at(1, -1), at(-1, 1), at(-1, -1)
-            sx, sy = xp + xm, yp + ym
-            a, b = pp + mm, pm + mp
-            sxy = a + b
-            if c < 2:
-                dxy = a - b
-                turn[c] = dxy
-            e, f = pp - mm, pm - mp
-            if c != 1:
-                dx_sy = e + f
-                dx = xp - xm
-            if c != 0:
-                dy_sx = e - f
-                dy = yp - ym
-            if c == 0:
-                even[0] = SIDE * u + EDGE * sx + FLAT * sy + sxy
-                flat[0] = FACE * sx + SIDE * sy + EDGE * sxy
-                sums.append((dx, dx_sy))
-            elif c == 1:
-                even[1] = SIDE * u + EDGE * sy + FLAT * sx + sxy
-                flat[1] = FACE * sy + SIDE * sx + EDGE * sxy
-                sums.append((dy, dy_sx))
-            else:
-                both = sx + sy
-                even[2] = FACE * u + EDGE * both + sxy
-                flat[2] = SIDE * both + FLAT * sxy
-                odd[0] = TURN * dx + TWIST * dx_sy
-                odd[1] = TURN * dy + TWIST * dy_sx
-        odd[2] = TURN * (sums[0][0] + sums[1][0]) + TWIST * (sums[0][1] + sums[1][1])
-        even[0] = even[0] + TWIST * turn[1]
-        flat[0] = flat[0] + TURN * turn[1]
-        even[1] = even[1] + TWIST * turn[0]
-        flat[1] = flat[1] + TURN * turn[0]
-        for c in range(3):
-            centre[c].append(flat[c])
-            above[c].append(even[c] + odd[c])
-            below[c].append(even[c] - odd[c])
-    return [join_lanes(centre[c], above[c], below[c]) for c in range(3)]
-
-
-def coupling(field, scaled, modulus, plane, row, tiles):
-    plain = stencil(field, plane, row, tiles)
-    heavy = stencil(scaled, plane, row, tiles)
-    return [[modulus[t] * plain[c][t] + heavy[c][t] for t in range(tiles)] for c in range(3)]
+            mids, sums, diffs = [], [], []
+            for p in range(count + 2):
+                u = field[c, plane + (p - 1), tile, pl.ds(row, 8), :]
+                yp = field[c, plane + (p - 1), tile, pl.ds(row + 1, 8), :]
+                ym = field[c, plane + (p - 1), tile, pl.ds(row - 1, 8), :]
+                mids.append(u)
+                sums.append(yp + ym)
+                diffs.append(yp - ym)
+            mid.append(mids)
+            summed.append(sums)
+            spread.append(diffs)
+        for p in range(count):
+            u, sy, dy = ([f[c][p + 1] for c in range(3)] for f in (mid, summed, spread))
+            sx = [mid[c][p + 2] + mid[c][p] for c in range(3)]
+            sxy = [summed[c][p + 2] + summed[c][p] for c in range(3)]
+            dxy = [spread[c][p + 2] - spread[c][p] for c in range(2)]
+            dx = {c: mid[c][p + 2] - mid[c][p] for c in (0, 2)}
+            dx_sy = {c: summed[c][p + 2] - summed[c][p] for c in (0, 2)}
+            dy_sx = {c: spread[c][p + 2] + spread[c][p] for c in (1, 2)}
+            both = sx[2] + sy[2]
+            flat = [
+                FACE * sx[0] + SIDE * sy[0] + EDGE * sxy[0] + TURN * dxy[1],
+                FACE * sy[1] + SIDE * sx[1] + EDGE * sxy[1] + TURN * dxy[0],
+                SIDE * both + FLAT * sxy[2],
+            ]
+            even = [
+                SIDE * u[0] + EDGE * sx[0] + FLAT * sy[0] + sxy[0] + TWIST * dxy[1],
+                SIDE * u[1] + EDGE * sy[1] + FLAT * sx[1] + sxy[1] + TWIST * dxy[0],
+                FACE * u[2] + EDGE * both + sxy[2],
+            ]
+            odd = [
+                TURN * dx[2] + TWIST * dx_sy[2],
+                TURN * dy[2] + TWIST * dy_sx[2],
+                TURN * (dx[0] + dy[1]) + TWIST * (dx_sy[0] + dy_sx[1]),
+            ]
+            for c in range(3):
+                centre[p][c].append(flat[c])
+                above[p][c].append(even[c] + odd[c])
+                below[p][c].append(even[c] - odd[c])
+    return [[join_lanes(centre[p][c], above[p][c], below[p][c]) for c in range(3)] for p in range(count)]
+
+
+def coupling(field, scaled, modulus, plane, count, row, tiles):
+    plain = stencil(field, plane, count, row, tiles)
+    part = [[[modulus[p][t] * plain[p][c][t] for t in range(tiles)] for c in range(3)] for p in range(count)]
+    heavy = stencil(scaled, plane, count, row, tiles)
+    return [[[part[p][c][t] + heavy[p][c][t] for t in range(tiles)] for c in range(3)] for p in range(count)]
+
+
+def sweep(planes, rows, tiles, now, later, fields, scale, kept_tiles=None, emit=None):
+    rest, modulus, diag, inverse = fields
+    kept_tiles = kept_tiles or tiles
+    lo, hi = planes
+    chunk = next(n for n in (4, 7, 6, 5, 2, 1) if (hi - lo) % n == 0)
+
+    def body(i, carry):
+        first = lo + i * chunk
+        for row in rows:
+            mod = [[modulus(first + j, t, row) for t in range(tiles)] for j in range(chunk)]
+            out = coupling(now[0], now[1], mod, first, chunk, 8 + row, tiles)
+            for j in range(chunk):
+                plane = first + j
+                for t in range(kept_tiles):
+                    d = diag(plane, t, row)
+                    if scale:
+                        inv = inverse(plane, t, row) * scale[1]
+                    for c in range(3):
+                        old = now[0][c, plane, t, pl.ds(8 + row, 8), :]
+                        r = rest[c, plane, t, pl.ds(row, 8), :] - d * old + out[j][c][t]
+                        if not emit:
+                            rest[c, plane, t, pl.ds(row, 8), :] = r
+                        if scale:
+                            step = inv * r
+                            if scale[0]:
+                                step = scale[0] * old + step
+                            if emit:
+                                emit(c, plane, step)
+                            else:
+                                later[0][c, plane, t, pl.ds(8 + row, 8), :] = step
+                                later[1][c, plane, t, pl.ds(8 + row, 8), :] = mod[j][t] * step
+        return carry
+
+    lax.fori_loop(0, (hi - lo) // chunk, body, 0)
 
 
 def diagonal(modulus, plane, row, tiles):
@@ -149,7 +183,7 @@
         last[c, 0] = tail
 
 
-def smooth_kernel(down, own, up, smooth, message, state, u, v, rest, modulus, diag, inverse, pairs):
+def smooth_kernel(down, own, up, smooth, message, state, ua, ub, va, vb, rest, modulus, diag, inverse, pairs):
     lane = lane_index()
     low, high = lane < HALO, lane >= 128 - HALO
 
@@ -179,8 +213,8 @@
                 inverse[plane, tile, pl.ds(8 * t, 8), :] = inv
                 for c in range(3):
                     step = rest[c, plane, tile, pl.ds(8 * t, 8), :] * (inv * (1.0 / THETA))
-                    u[0, c, plane, tile, pl.ds(8 + 8 * t, 8), :] = step
-                    v[0, c, plane, tile, pl.ds(8 + 8 * t, 8), :] = mid * step
+                    ua[c, plane, tile, pl.ds(8 + 8 * t, 8), :] = step
+                    va[c, plane, tile, pl.ds(8 + 8 * t, 8), :] = mid * step
         return carry
 
     lax.fori_loop(1, 23, begin, 0)
@@ -188,40 +222,25 @@
     def gather(slot, start):
         def body(p, carry):
             for c in range(3):
-                step = u[slot, c, 8 + p, 0, pl.ds(16, 8), :]
+                step = slot[c, 8 + p, 0, pl.ds(16, 8), :]
                 smooth[c, p] = step if start else smooth[c, p] + step
             return carry
 
         lax.fori_loop(0, 8, body, 0)
 
-    gather(0, True)
+    gather(ua, True)
     scales = sweep_scales()
+
+    def plain(ref, margin):
+        return lambda plane, tile, row: ref[plane, tile, pl.ds(margin + row, 8), :]
+
+    fields = (rest, plain(modulus, 8), plain(diag, 0), plain(inverse, 0))
     for k in range(1, SWEEPS + 1):
-        now, later = (k - 1) % 2, k % 2
-        rows = (0, 8, 16) if k < 3 else (4, 12)
-
-        def sweep(plane, carry, k=k, now=now, later=later, rows=rows):
-            for row in rows:
-                mod = [modulus[plane, tile, pl.ds(8 + row, 8), :] for tile in range(2)]
-                out = coupling(u.at[now], v.at[now], mod, plane, 8 + row, 2)
-                for tile in range(2):
-                    d = diag[plane, tile, pl.ds(row, 8), :]
-                    if k < SWEEPS:
-                        keep, push = scales[k - 1]
-                        inv = inverse[plane, tile, pl.ds(row, 8), :] * push
-                    for c in range(3):
-                        old = u[now, c, plane, tile, pl.ds(8 + row, 8), :]
-                        r = rest[c, plane, tile, pl.ds(row, 8), :] - d * old + out[c][tile]
-                        rest[c, plane, tile, pl.ds(row, 8), :] = r
-                        if k < SWEEPS:
-                            step = keep * old + inv * r
-                            u[later, c, plane, tile, pl.ds(8 + row, 8), :] = step
-                            v[later, c, plane, tile, pl.ds(8 + row, 8), :] = mod[tile] * step
-            return carry
-
-        lax.fori_loop(1 + k if k < SWEEPS else 5, 23 - k if k < SWEEPS else 19, sweep, 0)
+        now, later = ((ua, va), (ub, vb)) if k % 2 else ((ub, vb), (ua, va))
+        planes = (1 + k, 23 - k) if k < SWEEPS else (5, 19)
+        sweep(planes, (0, 8, 16) if k < 3 else (4, 12), 2, now, later, fields, scales[k - 1] if k < SWEEPS else None)
         if k < SWEEPS:
-            gather(later, False)
+            gather(later[0], False)
 
     def restrict(p, carry):
         for tile in range(2):
@@ -264,7 +283,7 @@
     lax.fori_loop(0, 16, keep_state, 0)
 
 
-def post_kernel(down, own, up, state, smooth, correction, coarse, cu, cv, crest, cmod, cinv, cdiag, total, u, v, wide):
+def post_kernel(down, own, up, state, smooth, correction, coarse, ca, cb, cva, cvb, crest, cmod, cinv, cdiag, total, ua, ub, va, vb, wide):
     scales = sweep_scales()
 
     def place(p, carry):
@@ -289,8 +308,8 @@
             cinv[plane, 0, pl.ds(8 * t, 8), :] = inv
             for c in range(3):
                 step = crest[c, plane, 0, pl.ds(8 * t, 8), :] * (inv * (1.0 / THETA))
-                cu[0, c, plane, 0, pl.ds(8 + 8 * t, 8), :] = step
-                cv[0, c, plane, 0, pl.ds(8 + 8 * t, 8), :] = mid * step
+                ca[c, plane, 0, pl.ds(8 + 8 * t, 8), :] = step
+                cva[c, plane, 0, pl.ds(8 + 8 * t, 8), :] = mid * step
         return carry
 
     lax.fori_loop(1, 15, begin, 0)
@@ -298,34 +317,22 @@
     def gather(slot, start):
         def body(p, carry):
             for c in range(3):
-                step = cu[slot, c, 4 + p, 0, pl.ds(12, 8), :]
+                step = slot[c, 4 + p, 0, pl.ds(12, 8), :]
                 total[c, p] = step if start else total[c, p] + step
             return carry
 
         lax.fori_loop(0, 8, body, 0)
 
-    gather(0, True)
+    gather(ca, True)
+
+    def plain(ref, margin):
+        return lambda plane, tile, row: ref[plane, tile, pl.ds(margin + row, 8), :]
+
+    fields = (crest, plain(cmod, 8), plain(cdiag, 0), plain(cinv, 0))
     for k in range(1, SWEEPS):
-        now, later = (k - 1) % 2, k % 2
-
-        def sweep(plane, carry, k=k, now=now, later=later):
-            for row in (0, 8):
-                mod = [cmod[plane, 0, pl.ds(8 + row, 8), :]]
-                out = coupling(cu.at[now], cv.at[now], mod, plane, 8 + row, 1)
-                d = cdiag[plane, 0, pl.ds(row, 8), :]
-                keep, push = scales[k - 1]
-                inv = cinv[plane, 0, pl.ds(row, 8), :] * push
-                for c in range(3):
-                    old = cu[now, c, plane, 0, pl.ds(8 + row, 8), :]
-                    r = crest[c, plane, 0, pl.ds(row, 8), :] - d * old + out[c][0]
-                    crest[c, plane, 0, pl.ds(row, 8), :] = r
-                    step = keep * old + inv * r
-                    cu[later, c, plane, 0, pl.ds(8 + row, 8), :] = step
-                    cv[later, c, plane, 0, pl.ds(8 + row, 8), :] = mod[0] * step
-            return carry
-
-        lax.fori_loop(1 + k, 15 - k, sweep, 0)
-        gather(later, False)
+        now, later = ((ca, cva), (cb, cvb)) if k % 2 else ((cb, cvb), (ca, cva))
+        sweep((1 + k, 15 - k), (0, 8), 1, now, later, fields, scales[k - 1])
+        gather(later[0], False)
 
     for c in range(3):
         for p in range(4):
@@ -347,7 +354,7 @@
                 value = wide[tile, c, p]
                 for dx in range(2):
                     for dy in range(2):
-                        u[0, c, 2 * p + dx, tile, pl.ds(8 + dy, 8, stride=2), :] = value
+                        ua[c, 2 * p + dx, tile, pl.ds(8 + dy, 8, stride=2), :] = value
         return carry
 
     lax.fori_loop(0, 8, lift, 0)
@@ -356,7 +363,7 @@
         for tile in range(2):
             mod = state[3, p, tile]
             for c in range(3):
-                v[0, c, p, tile, pl.ds(8, 16), :] = mod * u[0, c, p, tile, pl.ds(8, 16), :]
+                va[c, p, tile, pl.ds(8, 16), :] = mod * ua[c, p, tile, pl.ds(8, 16), :]
         return carry
 
     lax.fori_loop(0, 16, weigh, 0)
@@ -364,42 +371,29 @@
     def add_own(slot, start):
         def body(p, carry):
             for c in range(3):
-                step = u[slot, c, 4 + p, 0, pl.ds(12, 8), :]
+                step = slot[c, 4 + p, 0, pl.ds(12, 8), :]
                 correction[c, p] = (smooth[c, p] if start else correction[c, p]) + step
             return carry
 
         lax.fori_loop(0, 8, body, 0)
 
-    add_own(0, True)
+    add_own(ua, True)
+
+    def held(index):
+        return lambda plane, tile, row: state[index, plane, tile, pl.ds(row, 8), :]
+
+    def emit(c, plane, step):
+        correction[c, plane - 4] = correction[c, plane - 4] + step
+
+    fields = (state, held(3), held(4), held(5))
     for k in range(SWEEPS):
-        now, later = k % 2, (k + 1) % 2
-        rows = (0, 8) if k < SWEEPS - 1 else (4,)
-
-        def sweep(plane, carry, k=k, now=now, later=later, rows=rows):
-            for row in rows:
-                mod = [state[3, plane, tile, pl.ds(row, 8), :] for tile in range(2)]
-                out = coupling(u.at[now], v.at[now], mod, plane, 8 + row, 2)
-                for tile in range(2 if k < SWEEPS - 1 else 1):
-                    d = state[4, plane, tile, pl.ds(row, 8), :]
-                    keep, push = scales[k - 1] if k else (None, 1.0 / THETA)
-                    inv = state[5, plane, tile, pl.ds(row, 8), :] * push
-                    for c in range(3):
-                        old = u[now, c, plane, tile, pl.ds(8 + row, 8), :]
-                        r = state[c, plane, tile, pl.ds(row, 8), :] - d * old + out[c][tile]
-                        step = inv * r
-                        if k:
-                            step = keep * old + step
-                        if k < SWEEPS - 1:
-                            state[c, plane, tile, pl.ds(row, 8), :] = r
-                            u[later, c, plane, tile, pl.ds(8 + row, 8), :] = step
-                            v[later, c, plane, tile, pl.ds(8 + row, 8), :] = mod[tile] * step
-                        else:
-                            correction[c, plane - 4] = correction[c, plane - 4] + step
-            return carry
-
-        lax.fori_loop(1 + k, 15 - k, sweep, 0)
+        now, later = ((ub, vb), (ua, va)) if k % 2 else ((ua, va), (ub, vb))
+        scale = scales[k - 1] if k else (None, 1.0 / THETA)
         if k < SWEEPS - 1:
-            add_own(later, False)
+            sweep((1 + k, 15 - k), (0, 8), 2, now, later, fields, scale)
+            add_own(later[0], False)
+        else:
+            sweep((1 + k, 15 - k), (4,), 2, now, None, fields, scale, 1, emit)
 
 
 def call(kernel, outs, scratch=(), aliases=None):
@@ -431,8 +425,7 @@
         smooth_kernel,
         [(3, 8, 8, 128), (4, 8, 8, 128), (6, 16, 2, 16, 128)],
         [
-            (2, 3, planes, 2, rows + 16, 128),
-            (2, 3, planes, 2, rows + 16, 128),
+            *[(3, planes, 2, rows + 16, 128)] * 4,
             (3, planes, 2, rows, 128),
             (planes, 2, rows + 16, 128),
             (planes, 2, rows, 128),
@@ -447,15 +440,13 @@
         functools.partial(post_outer),
         [(3, 8, 8, 128), (3, 4, 4, 64)],
         [
-            (2, 3, 16, 1, 32, 128),
-            (2, 3, 16, 1, 32, 128),
+            *[(3, 16, 1, 32, 128)] * 4,
             (3, 16, 1, 16, 128),
             (16, 1, 32, 128),
             (16, 1, 16, 128),
             (16, 1, 16, 128),
             (3, 8, 8, 128),
-            (2, 3, 16, 2, 32, 128),
-            (2, 3, 16, 2, 32, 128),
+            *[(3, 16, 2, 32, 128)] * 4,
             (2, 3, 8, 8, 128),
             (6, 16, 2, 16, 128),
         ],

time: 96.5 us -> 87.6 us (0.908)
  Pallas kernels: 34.6 us -> 25.6 us
    pallas_call x1, Pallas kernels: 16.4 us -> 10.6 us  [on_device(): call(functools.partial(post_outer), [(3, 8, 8, 128), (3, 4, 4, 64)], [*[(...]
    pallas_call x1, Pallas kernels: 18 us -> 14.9 us  [on_device(): call(smooth_kernel, [(3, 8, 8, 128), (4, 8, 8, 128), (6, 16, 2, 16, 128)]...]
where the time goes in v1:
time: 87.6 us; the launch traced here: 87.1 us
  waiting for transfers between devices  32.6 us (37%)
  starting transfers between devices  26.4 us (30%)
  Pallas kernels  25.6 us (29%)
  local copies, waits for them, and re-layouts  1.68 us (2%)
    ppermute x5, waiting for transfers between devices, neighbours(): lax.ppermute(to_previous, axis, [(i + 1, i) for i in range(count - 1)])  19.4 us
    ppermute x5, starting transfers between devices, neighbours(): before = lax.ppermute(to_next, axis, [(i, i + 1) for i in range(count - 1)])  17 us
    pallas_call x1, Pallas kernels, on_device(): call(smooth_kernel, [(3, 8, 8, 128), (4, 8, 8, 128), (6, 16, 2, 16, 128)]...  14.9 us
    ppermute x5, waiting for transfers between devices, neighbours(): before = lax.ppermute(to_next, axis, [(i, i + 1) for i in range(count - 1)])  13.2 us
    pallas_call x1, Pallas kernels, on_device(): call(functools.partial(post_outer), [(3, 8, 8, 128), (3, 4, 4, 64)], [*[(...  10.6 us
    ppermute x5, starting transfers between devices, neighbours(): lax.ppermute(to_previous, axis, [(i + 1, i) for i in range(count - 1)])  9.4 us
  transfers between devices with their start and end apart: 10, of which 9 were waited for; matrix products, arithmetic and copies ran while one was open for 0% of the time, Pallas kernels for 0%

profile of v1, /device:TPU:288, one launch (start us, length us, event | category | flops | bytes accessed | tf_op | source)
XLA Modules:
  0.0 87.1 jit_solution(16429669593860284567)
XLA Ops:
  0.6 0.9 %copy-done = f32[3,8,8,128]{3,2,1,0:T(8,128)S(1)} copy-done((f32[3,8,8,128]{3,2,1,0:T(8,128)S(1)}, f32[3,8,8,128]{3,2,1,0:T(8,128)}, u32[]{:S(2)}) %copy-start) | copy-done | bytes 98328
  1.5 0.8 copy-done.1
  2.3 0.1 shard_map.41
  2.4 1.7 %collective-permute-start = (f32[4,1,8,128]{3,2,1,0:T(8,128)S(1)}, f32[4,1,8,128]{3,2,1,0:T(8,128)S(1)}, u32[]{:S(2)}, u32[]{:S(2)}) collective-permute-start(f32[4,1,8,128]{3,2,1,0:T(8,128)S(1)} %get-tuple-element.9), channel_id=1, source_target_pairs={{0,1},{1,2},{2,3},{3,4},{4,5},{5,6},{6,7},{8,9},{9,10},{10,11},{11... | collective-permute-start | bytes 49160 | tf_op jit(solution)/shard_map/ppermute | solution.py:411
  4.2 1.3 %collective-permute-start.1 = (f32[4,1,8,128]{3,2,1,0:T(8,128)S(1)}, f32[4,1,8,128]{3,2,1,0:T(8,128)S(1)}, u32[]{:S(2)}, u32[]{:S(2)}) collective-permute-start(f32[4,1,8,128]{3,2,1,0:T(8,128)S(1)} %get-tuple-element.10), channel_id=1, source_target_pairs={{1,0},{2,1},{3,2},{4,3},{5,4},{6,5},{7,6},{9,8},{10,9},{11,10},{12... | collective-permute-start | bytes 49160 | tf_op jit(solution)/shard_map/ppermute | solution.py:412
  5.5 3.0 %collective-permute-done.1 = f32[4,1,8,128]{3,2,1,0:T(8,128)S(1)} collective-permute-done((f32[4,1,8,128]{3,2,1,0:T(8,128)S(1)}, f32[4,1,8,128]{3,2,1,0:T(8,128)S(1)}, u32[]{:S(2)}, u32[]{:S(2)}) %collective-permute-start.1) | collective-permute-done | bytes 16416 | tf_op jit(solution)/shard_map/ppermute | solution.py:412
  8.5 1.9 %collective-permute-start.3 = (f32[4,10,8,128]{3,2,1,0:T(8,128)S(1)}, f32[4,10,8,128]{3,2,1,0:T(8,128)S(1)}, u32[]{:S(2)}, u32[]{:S(2)}) collective-permute-start(f32[4,10,8,128]{3,2,1,0:T(8,128)S(1)} %constant_dynamic-update-slice_fusion), channel_id=1, source_target_pairs={{64,0},{128,64},{192,128},{256,192},{320,256},{384,320},{448,384},... | collective-permute-start | bytes 491528 | tf_op jit(solution)/shard_map/ppermute | solution.py:412
  10.4 3.9 %collective-permute-start.2 = (f32[4,10,8,128]{3,2,1,0:T(8,128)S(1)}, f32[4,10,8,128]{3,2,1,0:T(8,128)S(1)}, u32[]{:S(2)}, u32[]{:S(2)}) collective-permute-start(f32[4,10,8,128]{3,2,1,0:T(8,128)S(1)} %constant_dynamic-update-slice_fusion), channel_id=1, source_target_pairs={{0,64},{64,128},{128,192},{192,256},{256,320},{320,384},{384,448},... | collective-permute-start | bytes 491528 | tf_op jit(solution)/shard_map/ppermute | solution.py:411
  14.4 1.5 %collective-permute-done.3 = f32[4,10,8,128]{3,2,1,0:T(8,128)S(1)} collective-permute-done((f32[4,10,8,128]{3,2,1,0:T(8,128)S(1)}, f32[4,10,8,128]{3,2,1,0:T(8,128)S(1)}, u32[]{:S(2)}, u32[]{:S(2)}) %collective-permute-start.3) | collective-permute-done | bytes 163872 | tf_op jit(solution)/shard_map/ppermute | solution.py:412
  15.9 3.1 %collective-permute-done.2 = f32[4,10,8,128]{3,2,1,0:T(8,128)S(1)} collective-permute-done((f32[4,10,8,128]{3,2,1,0:T(8,128)S(1)}, f32[4,10,8,128]{3,2,1,0:T(8,128)S(1)}, u32[]{:S(2)}, u32[]{:S(2)}) %collective-permute-start.2) | collective-permute-done | bytes 163872 | tf_op jit(solution)/shard_map/ppermute | solution.py:411
  19.1 2.4 %collective-permute-start.5 = (f32[3,4,10,8,128]{4,3,2,1,0:T(8,128)S(1)}, f32[3,4,10,8,128]{4,3,2,1,0:T(8,128)S(1)}, u32[]{:S(2)}, u32[]{:S(2)}) collective-permute-start(f32[3,4,10,8,128]{4,3,2,1,0:T(8,128)S(1)} %pad_maximum_fusion.own), channel_id=1, source_target_pairs={{8,0},{16,8},{24,16},{32,24},{40,32},{48,40},{56,48},{9,1},{17,9},... | collective-permute-start | bytes 1474568 | tf_op jit(solution)/shard_map/ppermute | solution.py:412
  21.4 3.5 %collective-permute-start.4 = (f32[3,4,10,8,128]{4,3,2,1,0:T(8,128)S(1)}, f32[3,4,10,8,128]{4,3,2,1,0:T(8,128)S(1)}, u32[]{:S(2)}, u32[]{:S(2)}) collective-permute-start(f32[3,4,10,8,128]{4,3,2,1,0:T(8,128)S(1)} %pad_maximum_fusion.own), channel_id=1, source_target_pairs={{0,8},{8,16},{16,24},{24,32},{32,40},{40,48},{48,56},{1,9},{9,17},... | collective-permute-start | bytes 1474568 | tf_op jit(solution)/shard_map/ppermute | solution.py:411
  24.9 9.8 %collective-permute-done.5.up = f32[3,4,10,8,128]{4,3,2,1,0:T(8,128)S(1)} collective-permute-done((f32[3,4,10,8,128]{4,3,2,1,0:T(8,128)S(1)}, f32[3,4,10,8,128]{4,3,2,1,0:T(8,128)S(1)}, u32[]{:S(2)}, u32[]{:S(2)}) %collective-permute-start.5) | collective-permute-done | bytes 491552 | tf_op jit(solution)/shard_map/ppermute | solution.py:412
  34.7 3.8 %collective-permute-done.4.down = f32[3,4,10,8,128]{4,3,2,1,0:T(8,128)S(1)} collective-permute-done((f32[3,4,10,8,128]{4,3,2,1,0:T(8,128)S(1)}, f32[3,4,10,8,128]{4,3,2,1,0:T(8,128)S(1)}, u32[]{:S(2)}, u32[]{:S(2)}) %collective-permute-start.4) | collective-permute-done | bytes 491552 | tf_op jit(solution)/shard_map/ppermute | solution.py:411
  38.5 14.9 %shard_map.42 = (f32[3,8,8,128]{3,2,1,0:T(8,128)S(1)}, f32[4,8,8,128]{3,2,1,0:T(8,128)S(1)}, f32[6,16,2,16,128]{4,3,2,1,0:T(8,128)S(1)}) custom-call(f32[3,4,10,8,128]{4,3,2,1,0:T(8,128)S(1)} %collective-permute-done.4.down, f32[3,4,10,8,128]{4,3,2,1,0:T(8,128)S(1)} %pad_maximum_fusion.own, f32[3,4,10,8,128]{4,3,2,1,0:T(8,128)S(1)} %collective-permute-done.5.up), custom_call_target="tpu_custom_call" | custom-call | tf_op jit(solution)/shard_map/pallas_call | solution.py:424
  53.4 1.9 %collective-permute-start.7 = (f32[4,8,8,128]{3,2,1,0:T(8,128)S(1)}, f32[4,8,8,128]{3,2,1,0:T(8,128)S(1)}, u32[]{:S(2)}, u32[]{:S(2)}) collective-permute-start(f32[4,8,8,128]{3,2,1,0:T(8,128)S(1)} %get-tuple-element.11), channel_id=1, source_target_pairs={{64,0},{128,64},{192,128},{256,192},{320,256},{384,320},{448,384},... | collective-permute-start | bytes 393224 | tf_op jit(solution)/shard_map/ppermute | solution.py:412
  55.4 3.9 %collective-permute-start.6 = (f32[4,8,8,128]{3,2,1,0:T(8,128)S(1)}, f32[4,8,8,128]{3,2,1,0:T(8,128)S(1)}, u32[]{:S(2)}, u32[]{:S(2)}) collective-permute-start(f32[4,8,8,128]{3,2,1,0:T(8,128)S(1)} %get-tuple-element.11), channel_id=1, source_target_pairs={{0,64},{64,128},{128,192},{192,256},{256,320},{320,384},{384,448},... | collective-permute-start | bytes 393224 | tf_op jit(solution)/shard_map/ppermute | solution.py:411
  59.3 1.5 %collective-permute-done.7 = f32[4,8,8,128]{3,2,1,0:T(8,128)S(1)} collective-permute-done((f32[4,8,8,128]{3,2,1,0:T(8,128)S(1)}, f32[4,8,8,128]{3,2,1,0:T(8,128)S(1)}, u32[]{:S(2)}, u32[]{:S(2)}) %collective-permute-start.7) | collective-permute-done | bytes 131104 | tf_op jit(solution)/shard_map/ppermute | solution.py:412
  60.8 3.1 %collective-permute-done.6 = f32[4,8,8,128]{3,2,1,0:T(8,128)S(1)} collective-permute-done((f32[4,8,8,128]{3,2,1,0:T(8,128)S(1)}, f32[4,8,8,128]{3,2,1,0:T(8,128)S(1)}, u32[]{:S(2)}, u32[]{:S(2)}) %collective-permute-start.6) | collective-permute-done | bytes 131104 | tf_op jit(solution)/shard_map/ppermute | solution.py:411
  64.0 1.9 %collective-permute-start.9 = (f32[4,16,8,128]{3,2,1,0:T(8,128)S(1)}, f32[4,16,8,128]{3,2,1,0:T(8,128)S(1)}, u32[]{:S(2)}, u32[]{:S(2)}) collective-permute-start(f32[4,16,8,128]{3,2,1,0:T(8,128)S(1)} %pad_maximum_fusion.1.own), channel_id=1, source_target_pairs={{8,0},{16,8},{24,16},{32,24},{40,32},{48,40},{56,48},{9,1},{17,9},... | collective-permute-start | bytes 786440 | tf_op jit(solution)/shard_map/ppermute | solution.py:412
  65.9 3.9 %collective-permute-start.8 = (f32[4,16,8,128]{3,2,1,0:T(8,128)S(1)}, f32[4,16,8,128]{3,2,1,0:T(8,128)S(1)}, u32[]{:S(2)}, u32[]{:S(2)}) collective-permute-start(f32[4,16,8,128]{3,2,1,0:T(8,128)S(1)} %pad_maximum_fusion.1.own), channel_id=1, source_target_pairs={{0,8},{8,16},{16,24},{24,32},{32,40},{40,48},{48,56},{1,9},{9,17},... | collective-permute-start | bytes 786440 | tf_op jit(solution)/shard_map/ppermute | solution.py:411
  69.9 3.5 %collective-permute-done.9.up = f32[4,16,8,128]{3,2,1,0:T(8,128)S(1)} collective-permute-done((f32[4,16,8,128]{3,2,1,0:T(8,128)S(1)}, f32[4,16,8,128]{3,2,1,0:T(8,128)S(1)}, u32[]{:S(2)}, u32[]{:S(2)}) %collective-permute-start.9) | collective-permute-done | bytes 262176 | tf_op jit(solution)/shard_map/ppermute | solution.py:412
  73.4 3.1 %collective-permute-done.8.down = f32[4,16,8,128]{3,2,1,0:T(8,128)S(1)} collective-permute-done((f32[4,16,8,128]{3,2,1,0:T(8,128)S(1)}, f32[4,16,8,128]{3,2,1,0:T(8,128)S(1)}, u32[]{:S(2)}, u32[]{:S(2)}) %collective-permute-start.8) | collective-permute-done | bytes 262176 | tf_op jit(solution)/shard_map/ppermute | solution.py:411
  76.5 10.6 %shard_map.43 = (f32[3,8,8,128]{3,2,1,0:T(8,128)}, f32[3,4,4,64]{3,2,1,0:T(4,128)}) custom-call(f32[4,16,8,128]{3,2,1,0:T(8,128)S(1)} %collective-permute-done.8.down, f32[4,16,8,128]{3,2,1,0:T(8,128)S(1)} %pad_maximum_fusion.1.own, f32[4,16,8,128]{3,2,1,0:T(8,128)S(1)} %collective-permute-done.9.up, f32[6,16,2,16,128]{4,3,2,1,0:T(8,128)S(1)} %get-tuple-element.12.state_in, ...), custom_call_target="tpu_custom_call" | custom-call | tf_op jit(solution)/shard_map/pallas_call | solution.py:439
  (11 shorter events, 0.1 us)
Async XLA Ops:
  0.6 0.9 %copy-start = (f32[3,8,8,128]{3,2,1,0:T(8,128)S(1)}, f32[3,8,8,128]{3,2,1,0:T(8,128)}, u32[]{:S(2)}) copy-start(f32[3,8,8,128]{3,2,1,0:T(8,128)} %residual.1) | copy-start | bytes 294916
  1.5 0.8 copy-start.1
  2.4 3.1 %collective-permute-start = (f32[4,1,8,128]{3,2,1,0:T(8,128)S(1)}, f32[4,1,8,128]{3,2,1,0:T(8,128)S(1)}, u32[]{:S(2)}, u32[]{:S(2)}) collective-permute-start(f32[4,1,8,128]{3,2,1,0:T(8,128)S(1)} %get-tuple-element.9), channel_id=1, source_target_pairs={{0,1},{1,2},{2,3},{3,4},{4,5},{5,6},{6,7},{8,9},{9,10},{10,11},{11... | collective-permute-start | bytes 49160 | tf_op jit(solution)/shard_map/ppermute | solution.py:411
  4.2 4.4 %collective-permute-start.1 = (f32[4,1,8,128]{3,2,1,0:T(8,128)S(1)}, f32[4,1,8,128]{3,2,1,0:T(8,128)S(1)}, u32[]{:S(2)}, u32[]{:S(2)}) collective-permute-start(f32[4,1,8,128]{3,2,1,0:T(8,128)S(1)} %get-tuple-element.10), channel_id=1, source_target_pairs={{1,0},{2,1},{3,2},{4,3},{5,4},{6,5},{7,6},{9,8},{10,9},{11,10},{12... | collective-permute-start | bytes 49160 | tf_op jit(solution)/shard_map/ppermute | solution.py:412
  8.5 7.4 %collective-permute-start.3 = (f32[4,10,8,128]{3,2,1,0:T(8,128)S(1)}, f32[4,10,8,128]{3,2,1,0:T(8,128)S(1)}, u32[]{:S(2)}, u32[]{:S(2)}) collective-permute-start(f32[4,10,8,128]{3,2,1,0:T(8,128)S(1)} %constant_dynamic-update-slice_fusion), channel_id=1, source_target_pairs={{64,0},{128,64},{192,128},{256,192},{320,256},{384,320},{448,384},... | collective-permute-start | bytes 491528 | tf_op jit(solution)/shard_map/ppermute | solution.py:412
  10.4 8.6 %collective-permute-start.2 = (f32[4,10,8,128]{3,2,1,0:T(8,128)S(1)}, f32[4,10,8,128]{3,2,1,0:T(8,128)S(1)}, u32[]{:S(2)}, u32[]{:S(2)}) collective-permute-start(f32[4,10,8,128]{3,2,1,0:T(8,128)S(1)} %constant_dynamic-update-slice_fusion), channel_id=1, source_target_pairs={{0,64},{64,128},{128,192},{192,256},{256,320},{320,384},{384,448},... | collective-permute-start | bytes 491528 | tf_op jit(solution)/shard_map/ppermute | solution.py:411
  19.1 15.6 %collective-permute-start.5 = (f32[3,4,10,8,128]{4,3,2,1,0:T(8,128)S(1)}, f32[3,4,10,8,128]{4,3,2,1,0:T(8,128)S(1)}, u32[]{:S(2)}, u32[]{:S(2)}) collective-permute-start(f32[3,4,10,8,128]{4,3,2,1,0:T(8,128)S(1)} %pad_maximum_fusion.own), channel_id=1, source_target_pairs={{8,0},{16,8},{24,16},{32,24},{40,32},{48,40},{56,48},{9,1},{17,9},... | collective-permute-start | bytes 1474568 | tf_op jit(solution)/shard_map/ppermute | solution.py:412
  21.4 17.1 %collective-permute-start.4 = (f32[3,4,10,8,128]{4,3,2,1,0:T(8,128)S(1)}, f32[3,4,10,8,128]{4,3,2,1,0:T(8,128)S(1)}, u32[]{:S(2)}, u32[]{:S(2)}) collective-permute-start(f32[3,4,10,8,128]{4,3,2,1,0:T(8,128)S(1)} %pad_maximum_fusion.own), channel_id=1, source_target_pairs={{0,8},{8,16},{16,24},{24,32},{32,40},{40,48},{48,56},{1,9},{9,17},... | collective-permute-start | bytes 1474568 | tf_op jit(solution)/shard_map/ppermute | solution.py:411
  53.4 7.4 %collective-permute-start.7 = (f32[4,8,8,128]{3,2,1,0:T(8,128)S(1)}, f32[4,8,8,128]{3,2,1,0:T(8,128)S(1)}, u32[]{:S(2)}, u32[]{:S(2)}) collective-permute-start(f32[4,8,8,128]{3,2,1,0:T(8,128)S(1)} %get-tuple-element.11), channel_id=1, source_target_pairs={{64,0},{128,64},{192,128},{256,192},{320,256},{384,320},{448,384},... | collective-permute-start | bytes 393224 | tf_op jit(solution)/shard_map/ppermute | solution.py:412
  55.4 8.6 %collective-permute-start.6 = (f32[4,8,8,128]{3,2,1,0:T(8,128)S(1)}, f32[4,8,8,128]{3,2,1,0:T(8,128)S(1)}, u32[]{:S(2)}, u32[]{:S(2)}) collective-permute-start(f32[4,8,8,128]{3,2,1,0:T(8,128)S(1)} %get-tuple-element.11), channel_id=1, source_target_pairs={{0,64},{64,128},{128,192},{192,256},{256,320},{320,384},{384,448},... | collective-permute-start | bytes 393224 | tf_op jit(solution)/shard_map/ppermute | solution.py:411
  64.0 9.4 %collective-permute-start.9 = (f32[4,16,8,128]{3,2,1,0:T(8,128)S(1)}, f32[4,16,8,128]{3,2,1,0:T(8,128)S(1)}, u32[]{:S(2)}, u32[]{:S(2)}) collective-permute-start(f32[4,16,8,128]{3,2,1,0:T(8,128)S(1)} %pad_maximum_fusion.1.own), channel_id=1, source_target_pairs={{8,0},{16,8},{24,16},{32,24},{40,32},{48,40},{56,48},{9,1},{17,9},... | collective-permute-start | bytes 786440 | tf_op jit(solution)/shard_map/ppermute | solution.py:412
  65.9 10.6 %collective-permute-start.8 = (f32[4,16,8,128]{3,2,1,0:T(8,128)S(1)}, f32[4,16,8,128]{3,2,1,0:T(8,128)S(1)}, u32[]{:S(2)}, u32[]{:S(2)}) collective-permute-start(f32[4,16,8,128]{3,2,1,0:T(8,128)S(1)} %pad_maximum_fusion.1.own), channel_id=1, source_target_pairs={{0,8},{8,16},{16,24},{24,32},{32,40},{40,48},{48,56},{1,9},{9,17},... | collective-permute-start | bytes 786440 | tf_op jit(solution)/shard_map/ppermute | solution.py:411
